TPU v7x, 32 devices: a whole 2x2x4 slice. The times are simulated.
32 devices in a mesh: rad: 8 (over z, y), lm: 4 (over x, core).
Axes of the slice: x: 2, y: 2, z: 4, core: 2. Of those that a mesh axis runs over, the one named last changes fastest.
Arguments:
- grid_field: bfloat16 [2, 512, 544, 128], P(None, ('rad', 'lm')), may hold values from -6 to 6
- inverses: bfloat16 [2, 64, 512, 512], P(None, ('rad', 'lm')), may hold values from -4 to 4
- slot_blocks: int32 [32, 24], replicated, may hold values from 0 to 544, as said below
- degree_start: int32 [64], replicated, may hold values from 0 to 752, as said below
Outputs:
- new_grid: bfloat16 [2, 512, 544, 128], P(None, ('rad', 'lm'))
- new_slope: bfloat16 [2, 512, 544, 128], P(None, ('rad', 'lm'))
Inputs may be any that keep to these rules, and one draw needn't show every extreme that they name: `slot_blocks`: row d lists the blocks of one degree index below 32 in order, then those of one degree index at or above it in order, then the value 544 (no block). Every block is in exactly one slot. `degree_start`: entry q equals d * 24 + s where slot s of row d of slot_blocks holds the first block of degree index q.
All inputs are finite; a program needn't handle non-finite values.
Results may differ from a plain program's by a relative error of at most 0.0052.
Values may be sent and summed in bfloat16 or wider, within the bound.
No kernel may reach another device: no remote copies, remote signals or barrier semaphores. Data moves between devices by JAX's collectives and lax.ppermute only.
A program may use at most 128 MiB of HBM per device.

v0:
```python
import jax
import jax.numpy as jnp
import numpy as np
from jax import lax
from jax.sharding import PartitionSpec as P

NR = 512
LMAX1 = 1024
OB = 64


inner_radius = 0.35
shell_depth = 0.65
diffusion_numbers = (0.9, 0.4)


def extended(value, sides, width):
    for axis, dim in sides:
        size, length = (lax.axis_size(axis), value.shape[dim])
        up = [(i, (i + 1) % size) for i in range(size - 1)]
        down = [(j, i) for i, j in up]
        last = lax.slice_in_dim(value, length - width, length, axis=dim)
        leading = lax.slice_in_dim(value, 0, width, axis=dim)
        before = lax.ppermute(last, axis, up)
        after = lax.ppermute(leading, axis, down)
        value = jnp.concatenate([before, value, after], axis=dim)
    return value


def block_tables(degrees, lmax_one, orders, blocks):
    spacing = lmax_one // degrees
    group_size = orders * degrees // lmax_one
    degree_index = np.arange(degrees)
    counts = degree_index // group_size + 1
    starts = np.cumsum(counts) - counts
    degree_of = np.repeat(degree_index, counts)
    place_in = np.arange(blocks) - starts[degree_of]
    degree_value = spacing * (degree_of + 1) - 1
    column = np.arange(2 * orders)
    live_mask = (place_in[:, None] * orders + column[None, :] // 2 <= degree_value[:, None]).astype(
        np.float32
    )
    factor = (degree_value * (degree_value + 1)).astype(np.float32)
    upper_half = (degree_of >= degrees // 2).astype(np.int32)
    return (degree_of.astype(np.int32), place_in.astype(np.int32), factor, live_mask, upper_half)


def radius_of(positions):
    return inner_radius + shell_depth * (positions + 1).astype(jnp.float32) / (NR + 1)


def right_side(padded, radius_list, factor, live_mask):
    spacing_h = shell_depth / (NR + 1)
    weighted = padded * radius_list[None, :, None, None]
    centre = padded[:, 1:-1]
    inner_radii = radius_list[1:-1][None, :, None, None]
    second = (weighted[:, 2:] - 2.0 * weighted[:, 1:-1] + weighted[:, :-2]) / inner_radii
    scaled = spacing_h / inner_radii
    angular = factor[None, None, :, None] * (scaled * scaled) * centre
    coefficient = jnp.array(diffusion_numbers, jnp.float32)[:, None, None, None]
    combined = centre + coefficient * (second - angular)
    return combined * live_mask[None, None]


def slope_from_padded(padded):
    return (0.5 * (padded[:, 2:].astype(jnp.float32) - padded[:, :-2].astype(jnp.float32))).astype(
        jnp.bfloat16
    )


def body(grid_field, inverses, slot_blocks, degree_start):
    rows_rad = lax.axis_size("rad")
    rows_lm = lax.axis_size("lm")
    devices = rows_rad * rows_lm
    fields, rad_local, blocks, width = grid_field.shape
    capacity = slot_blocks.shape[1]
    degree_of, place_in, factor, live_mask, upper_half = block_tables(
        2 * devices, LMAX1, OB, blocks
    )
    device = lax.axis_index(("rad", "lm"))
    chosen = lax.dynamic_index_in_dim(slot_blocks, device, 0, keepdims=False)
    positions = device * rad_local + jnp.arange(rad_local + 2, dtype=jnp.int32) - 1
    radius_list = radius_of(positions)
    padded = extended(grid_field, ((("rad", "lm"), 1),), 1)
    source = right_side(
        padded.astype(jnp.float32), radius_list, jnp.asarray(factor), jnp.asarray(live_mask)
    )
    packed = jnp.take(source, slot_blocks.reshape(-1), axis=2, mode="fill", fill_value=0.0)
    outgoing = packed.reshape(fields, 1, rad_local, devices, capacity, width)
    arrived = lax.all_to_all(outgoing, ("rad", "lm"), split_axis=3, concat_axis=1, tiled=True)
    columns = arrived.reshape(fields, NR, capacity, width)
    upper_pick = jnp.take(jnp.asarray(upper_half), chosen, mode="fill", fill_value=0)

    def solve_slot(slot_index, solved):
        block_rhs = lax.dynamic_index_in_dim(columns, slot_index, 2, keepdims=False)
        matrix = lax.dynamic_index_in_dim(
            inverses, upper_pick[slot_index], 1, keepdims=False
        ).astype(jnp.float32)
        product = jnp.einsum("fij,fjc->fic", matrix, block_rhs, precision=lax.Precision.HIGHEST)
        return lax.dynamic_update_index_in_dim(solved, product, slot_index, 2)

    solved = lax.fori_loop(0, capacity, solve_slot, jnp.zeros_like(columns))
    spectral = solved.astype(jnp.bfloat16)
    slot_place = jnp.take(degree_start, jnp.asarray(degree_of)) + jnp.asarray(place_in)
    outgoing_back = spectral.reshape(fields, devices, rad_local, 1, capacity, width)
    returned = lax.all_to_all(outgoing_back, ("rad", "lm"), split_axis=1, concat_axis=3, tiled=True)
    flat_slots = returned.reshape(fields, rad_local, devices * capacity, width)
    new_grid = jnp.take(flat_slots, slot_place, axis=2)
    rimmed = extended(new_grid, ((("rad", "lm"), 1),), 1)
    new_slope = slope_from_padded(rimmed)
    return (new_grid, new_slope)


def solution(mesh):
    in_specs = (P(None, ("rad", "lm"), None, None), P(None, ("rad", "lm"), None, None), P(), P())
    out_specs = (P(None, ("rad", "lm"), None, None), P(None, ("rad", "lm"), None, None))
    return jax.shard_map(body, mesh=mesh, in_specs=in_specs, out_specs=out_specs, check_vma=False)
```

profile of v0, /device:TPU:15, one launch (start us, length us, event | category | flops | bytes accessed | tf_op | source)
XLA Modules:
  0.0 1051.7 jit_solution(14593863138075188231)
XLA Ops:
  1.7 3.7 collective-permute-start
  9.1 6.1 copy.55
  16.3 6.0 broadcast_multiply_fusion
  22.4 6.7 maximum_convert_fusion
  29.2 10.4 fusion.8
  39.5 10.8 %gather_fusion.1 = f32[768,2,16,128]{3,2,1,0:T(8,128)} fusion(f32[2,16,544,128]{3,1,2,0:T(8,128)} %fusion.8, s32[1024]{0:T(1024)S(1)} %pad_clamp_fusion.1), kind=kCustom, calls=%fused_computation.1 | custom fusion | bytes 25168896 | tf_op jit(solution)/shard_map/jit(_take)/gather | solution.py:88
  50.3 10.3 broadcast_select_fusion
  60.6 6.6 all-to-all-start
  68.1 269.6 %all-to-all-done = f32[2,1,16,32,24,128]{5,2,0,4,1,3:T(8,128)} async-done(((f32[2,1,16,32,24,128]{5,2,0,4,1,3:T(8,128)}), f32[2,1,16,32,24,128]{5,2,0,4,1,3:T(8,128)}, u32[]{:S(2)}, u32[]{:S(2)}) %all-to-all-start) | async-done | bytes 12582944 | tf_op jit(solution)/shard_map/all_to_all | solution.py:90
  337.7 16.4 %copy.59 = f32[2,1,16,32,24,128]{5,4,2,3,0,1:T(8,128)} copy(f32[2,1,16,32,24,128]{5,2,0,4,1,3:T(8,128)} %all-to-all-done) | data formatting | bytes 25165824 | tf_op jit(solution)/shard_map/all_to_all | solution.py:90
  354.2 497.4 %while.13 = (s32[]{:T(128)}, bf16[2,512,24,128]{3,2,1,0:T(8,128)(2,1)}, s32[24]{0:T(128)S(1)}, bf16[2,2,512,512]{3,2,1,0:T(8,128)(2,1)S(1)}, f32[2,512,24,128]{3...) while((s32[]{:T(128)}, bf16[2,512,24,128]{3,2,1,0:T(8,128)(2,1)}, s32[24]{0:T(128)S(1)}, ...), condition=%wide.region_1.2_spmd, body=%wide.region_0.1_spmd.sunk | while | flops 805306368 | bytes 4194447 | solution.py:102
  356.7 2.6 constant_dynamic-slice_fusion.2
  360.4 14.6 %dynamic_update_slice.9 = bf16[2,512,24,128]{3,2,1,0:T(8,128)(2,1)} dynamic-update-slice(bf16[2,512,24,128]{3,2,1,0:T(8,128)(2,1)} %get-tuple-element.252, f32[2,512,1,128]{3,2,1,0:T(1,128)S(1)} %bitcast.109, s32[]{:T(128)} %constant.124.clone.1..sunk, s32[]{:T(128)} %constant.124.clone.1..sunk, s32[]{:T(128)} %get-tuple-element.251, s32[]{:T(128)} %constant.124.clone.1..sunk) | dynamic-update-slice | bytes 1048580 | tf_op jit(solution)/shard_map/while/body/eval_jaxpr/jit(dynamic_update_index_in_dim)/dynamic_update_slice | solution.py:100
  381.1 14.6 %dynamic_update_slice.9 = bf16[2,512,24,128]{3,2,1,0:T(8,128)(2,1)} dynamic-update-slice(bf16[2,512,24,128]{3,2,1,0:T(8,128)(2,1)} %get-tuple-element.252, f32[2,512,1,128]{3,2,1,0:T(1,128)S(1)} %bitcast.109, s32[]{:T(128)} %constant.124.clone.1..sunk, s32[]{:T(128)} %constant.124.clone.1..sunk, s32[]{:T(128)} %get-tuple-element.251, s32[]{:T(128)} %constant.124.clone.1..sunk) | dynamic-update-slice | bytes 1048580 | tf_op jit(solution)/shard_map/while/body/eval_jaxpr/jit(dynamic_update_index_in_dim)/dynamic_update_slice | solution.py:100
  401.9 14.6 %dynamic_update_slice.9 = bf16[2,512,24,128]{3,2,1,0:T(8,128)(2,1)} dynamic-update-slice(bf16[2,512,24,128]{3,2,1,0:T(8,128)(2,1)} %get-tuple-element.252, f32[2,512,1,128]{3,2,1,0:T(1,128)S(1)} %bitcast.109, s32[]{:T(128)} %constant.124.clone.1..sunk, s32[]{:T(128)} %constant.124.clone.1..sunk, s32[]{:T(128)} %get-tuple-element.251, s32[]{:T(128)} %constant.124.clone.1..sunk) | dynamic-update-slice | bytes 1048580 | tf_op jit(solution)/shard_map/while/body/eval_jaxpr/jit(dynamic_update_index_in_dim)/dynamic_update_slice | solution.py:100
  422.7 14.6 %dynamic_update_slice.9 = bf16[2,512,24,128]{3,2,1,0:T(8,128)(2,1)} dynamic-update-slice(bf16[2,512,24,128]{3,2,1,0:T(8,128)(2,1)} %get-tuple-element.252, f32[2,512,1,128]{3,2,1,0:T(1,128)S(1)} %bitcast.109, s32[]{:T(128)} %constant.124.clone.1..sunk, s32[]{:T(128)} %constant.124.clone.1..sunk, s32[]{:T(128)} %get-tuple-element.251, s32[]{:T(128)} %constant.124.clone.1..sunk) | dynamic-update-slice | bytes 1048580 | tf_op jit(solution)/shard_map/while/body/eval_jaxpr/jit(dynamic_update_index_in_dim)/dynamic_update_slice | solution.py:100
  443.4 14.6 %dynamic_update_slice.9 = bf16[2,512,24,128]{3,2,1,0:T(8,128)(2,1)} dynamic-update-slice(bf16[2,512,24,128]{3,2,1,0:T(8,128)(2,1)} %get-tuple-element.252, f32[2,512,1,128]{3,2,1,0:T(1,128)S(1)} %bitcast.109, s32[]{:T(128)} %constant.124.clone.1..sunk, s32[]{:T(128)} %constant.124.clone.1..sunk, s32[]{:T(128)} %get-tuple-element.251, s32[]{:T(128)} %constant.124.clone.1..sunk) | dynamic-update-slice | bytes 1048580 | tf_op jit(solution)/shard_map/while/body/eval_jaxpr/jit(dynamic_update_index_in_dim)/dynamic_update_slice | solution.py:100
  464.2 14.6 %dynamic_update_slice.9 = bf16[2,512,24,128]{3,2,1,0:T(8,128)(2,1)} dynamic-update-slice(bf16[2,512,24,128]{3,2,1,0:T(8,128)(2,1)} %get-tuple-element.252, f32[2,512,1,128]{3,2,1,0:T(1,128)S(1)} %bitcast.109, s32[]{:T(128)} %constant.124.clone.1..sunk, s32[]{:T(128)} %constant.124.clone.1..sunk, s32[]{:T(128)} %get-tuple-element.251, s32[]{:T(128)} %constant.124.clone.1..sunk) | dynamic-update-slice | bytes 1048580 | tf_op jit(solution)/shard_map/while/body/eval_jaxpr/jit(dynamic_update_index_in_dim)/dynamic_update_slice | solution.py:100
  485.0 14.6 %dynamic_update_slice.9 = bf16[2,512,24,128]{3,2,1,0:T(8,128)(2,1)} dynamic-update-slice(bf16[2,512,24,128]{3,2,1,0:T(8,128)(2,1)} %get-tuple-element.252, f32[2,512,1,128]{3,2,1,0:T(1,128)S(1)} %bitcast.109, s32[]{:T(128)} %constant.124.clone.1..sunk, s32[]{:T(128)} %constant.124.clone.1..sunk, s32[]{:T(128)} %get-tuple-element.251, s32[]{:T(128)} %constant.124.clone.1..sunk) | dynamic-update-slice | bytes 1048580 | tf_op jit(solution)/shard_map/while/body/eval_jaxpr/jit(dynamic_update_index_in_dim)/dynamic_update_slice | solution.py:100
  505.8 14.6 %dynamic_update_slice.9 = bf16[2,512,24,128]{3,2,1,0:T(8,128)(2,1)} dynamic-update-slice(bf16[2,512,24,128]{3,2,1,0:T(8,128)(2,1)} %get-tuple-element.252, f32[2,512,1,128]{3,2,1,0:T(1,128)S(1)} %bitcast.109, s32[]{:T(128)} %constant.124.clone.1..sunk, s32[]{:T(128)} %constant.124.clone.1..sunk, s32[]{:T(128)} %get-tuple-element.251, s32[]{:T(128)} %constant.124.clone.1..sunk) | dynamic-update-slice | bytes 1048580 | tf_op jit(solution)/shard_map/while/body/eval_jaxpr/jit(dynamic_update_index_in_dim)/dynamic_update_slice | solution.py:100
  526.5 14.6 %dynamic_update_slice.9 = bf16[2,512,24,128]{3,2,1,0:T(8,128)(2,1)} dynamic-update-slice(bf16[2,512,24,128]{3,2,1,0:T(8,128)(2,1)} %get-tuple-element.252, f32[2,512,1,128]{3,2,1,0:T(1,128)S(1)} %bitcast.109, s32[]{:T(128)} %constant.124.clone.1..sunk, s32[]{:T(128)} %constant.124.clone.1..sunk, s32[]{:T(128)} %get-tuple-element.251, s32[]{:T(128)} %constant.124.clone.1..sunk) | dynamic-update-slice | bytes 1048580 | tf_op jit(solution)/shard_map/while/body/eval_jaxpr/jit(dynamic_update_index_in_dim)/dynamic_update_slice | solution.py:100
  547.2 14.6 %dynamic_update_slice.9 = bf16[2,512,24,128]{3,2,1,0:T(8,128)(2,1)} dynamic-update-slice(bf16[2,512,24,128]{3,2,1,0:T(8,128)(2,1)} %get-tuple-element.252, f32[2,512,1,128]{3,2,1,0:T(1,128)S(1)} %bitcast.109, s32[]{:T(128)} %constant.124.clone.1..sunk, s32[]{:T(128)} %constant.124.clone.1..sunk, s32[]{:T(128)} %get-tuple-element.251, s32[]{:T(128)} %constant.124.clone.1..sunk) | dynamic-update-slice | bytes 1048580 | tf_op jit(solution)/shard_map/while/body/eval_jaxpr/jit(dynamic_update_index_in_dim)/dynamic_update_slice | solution.py:100
  567.8 14.6 %dynamic_update_slice.9 = bf16[2,512,24,128]{3,2,1,0:T(8,128)(2,1)} dynamic-update-slice(bf16[2,512,24,128]{3,2,1,0:T(8,128)(2,1)} %get-tuple-element.252, f32[2,512,1,128]{3,2,1,0:T(1,128)S(1)} %bitcast.109, s32[]{:T(128)} %constant.124.clone.1..sunk, s32[]{:T(128)} %constant.124.clone.1..sunk, s32[]{:T(128)} %get-tuple-element.251, s32[]{:T(128)} %constant.124.clone.1..sunk) | dynamic-update-slice | bytes 1048580 | tf_op jit(solution)/shard_map/while/body/eval_jaxpr/jit(dynamic_update_index_in_dim)/dynamic_update_slice | solution.py:100
  588.5 14.6 %dynamic_update_slice.9 = bf16[2,512,24,128]{3,2,1,0:T(8,128)(2,1)} dynamic-update-slice(bf16[2,512,24,128]{3,2,1,0:T(8,128)(2,1)} %get-tuple-element.252, f32[2,512,1,128]{3,2,1,0:T(1,128)S(1)} %bitcast.109, s32[]{:T(128)} %constant.124.clone.1..sunk, s32[]{:T(128)} %constant.124.clone.1..sunk, s32[]{:T(128)} %get-tuple-element.251, s32[]{:T(128)} %constant.124.clone.1..sunk) | dynamic-update-slice | bytes 1048580 | tf_op jit(solution)/shard_map/while/body/eval_jaxpr/jit(dynamic_update_index_in_dim)/dynamic_update_slice | solution.py:100
  609.2 14.6 %dynamic_update_slice.9 = bf16[2,512,24,128]{3,2,1,0:T(8,128)(2,1)} dynamic-update-slice(bf16[2,512,24,128]{3,2,1,0:T(8,128)(2,1)} %get-tuple-element.252, f32[2,512,1,128]{3,2,1,0:T(1,128)S(1)} %bitcast.109, s32[]{:T(128)} %constant.124.clone.1..sunk, s32[]{:T(128)} %constant.124.clone.1..sunk, s32[]{:T(128)} %get-tuple-element.251, s32[]{:T(128)} %constant.124.clone.1..sunk) | dynamic-update-slice | bytes 1048580 | tf_op jit(solution)/shard_map/while/body/eval_jaxpr/jit(dynamic_update_index_in_dim)/dynamic_update_slice | solution.py:100
  629.9 14.6 %dynamic_update_slice.9 = bf16[2,512,24,128]{3,2,1,0:T(8,128)(2,1)} dynamic-update-slice(bf16[2,512,24,128]{3,2,1,0:T(8,128)(2,1)} %get-tuple-element.252, f32[2,512,1,128]{3,2,1,0:T(1,128)S(1)} %bitcast.109, s32[]{:T(128)} %constant.124.clone.1..sunk, s32[]{:T(128)} %constant.124.clone.1..sunk, s32[]{:T(128)} %get-tuple-element.251, s32[]{:T(128)} %constant.124.clone.1..sunk) | dynamic-update-slice | bytes 1048580 | tf_op jit(solution)/shard_map/while/body/eval_jaxpr/jit(dynamic_update_index_in_dim)/dynamic_update_slice | solution.py:100
  650.6 14.6 %dynamic_update_slice.9 = bf16[2,512,24,128]{3,2,1,0:T(8,128)(2,1)} dynamic-update-slice(bf16[2,512,24,128]{3,2,1,0:T(8,128)(2,1)} %get-tuple-element.252, f32[2,512,1,128]{3,2,1,0:T(1,128)S(1)} %bitcast.109, s32[]{:T(128)} %constant.124.clone.1..sunk, s32[]{:T(128)} %constant.124.clone.1..sunk, s32[]{:T(128)} %get-tuple-element.251, s32[]{:T(128)} %constant.124.clone.1..sunk) | dynamic-update-slice | bytes 1048580 | tf_op jit(solution)/shard_map/while/body/eval_jaxpr/jit(dynamic_update_index_in_dim)/dynamic_update_slice | solution.py:100
  671.3 14.6 %dynamic_update_slice.9 = bf16[2,512,24,128]{3,2,1,0:T(8,128)(2,1)} dynamic-update-slice(bf16[2,512,24,128]{3,2,1,0:T(8,128)(2,1)} %get-tuple-element.252, f32[2,512,1,128]{3,2,1,0:T(1,128)S(1)} %bitcast.109, s32[]{:T(128)} %constant.124.clone.1..sunk, s32[]{:T(128)} %constant.124.clone.1..sunk, s32[]{:T(128)} %get-tuple-element.251, s32[]{:T(128)} %constant.124.clone.1..sunk) | dynamic-update-slice | bytes 1048580 | tf_op jit(solution)/shard_map/while/body/eval_jaxpr/jit(dynamic_update_index_in_dim)/dynamic_update_slice | solution.py:100
  692.0 14.6 %dynamic_update_slice.9 = bf16[2,512,24,128]{3,2,1,0:T(8,128)(2,1)} dynamic-update-slice(bf16[2,512,24,128]{3,2,1,0:T(8,128)(2,1)} %get-tuple-element.252, f32[2,512,1,128]{3,2,1,0:T(1,128)S(1)} %bitcast.109, s32[]{:T(128)} %constant.124.clone.1..sunk, s32[]{:T(128)} %constant.124.clone.1..sunk, s32[]{:T(128)} %get-tuple-element.251, s32[]{:T(128)} %constant.124.clone.1..sunk) | dynamic-update-slice | bytes 1048580 | tf_op jit(solution)/shard_map/while/body/eval_jaxpr/jit(dynamic_update_index_in_dim)/dynamic_update_slice | solution.py:100
  712.7 14.6 %dynamic_update_slice.9 = bf16[2,512,24,128]{3,2,1,0:T(8,128)(2,1)} dynamic-update-slice(bf16[2,512,24,128]{3,2,1,0:T(8,128)(2,1)} %get-tuple-element.252, f32[2,512,1,128]{3,2,1,0:T(1,128)S(1)} %bitcast.109, s32[]{:T(128)} %constant.124.clone.1..sunk, s32[]{:T(128)} %constant.124.clone.1..sunk, s32[]{:T(128)} %get-tuple-element.251, s32[]{:T(128)} %constant.124.clone.1..sunk) | dynamic-update-slice | bytes 1048580 | tf_op jit(solution)/shard_map/while/body/eval_jaxpr/jit(dynamic_update_index_in_dim)/dynamic_update_slice | solution.py:100
  733.4 14.6 %dynamic_update_slice.9 = bf16[2,512,24,128]{3,2,1,0:T(8,128)(2,1)} dynamic-update-slice(bf16[2,512,24,128]{3,2,1,0:T(8,128)(2,1)} %get-tuple-element.252, f32[2,512,1,128]{3,2,1,0:T(1,128)S(1)} %bitcast.109, s32[]{:T(128)} %constant.124.clone.1..sunk, s32[]{:T(128)} %constant.124.clone.1..sunk, s32[]{:T(128)} %get-tuple-element.251, s32[]{:T(128)} %constant.124.clone.1..sunk) | dynamic-update-slice | bytes 1048580 | tf_op jit(solution)/shard_map/while/body/eval_jaxpr/jit(dynamic_update_index_in_dim)/dynamic_update_slice | solution.py:100
  754.2 14.6 %dynamic_update_slice.9 = bf16[2,512,24,128]{3,2,1,0:T(8,128)(2,1)} dynamic-update-slice(bf16[2,512,24,128]{3,2,1,0:T(8,128)(2,1)} %get-tuple-element.252, f32[2,512,1,128]{3,2,1,0:T(1,128)S(1)} %bitcast.109, s32[]{:T(128)} %constant.124.clone.1..sunk, s32[]{:T(128)} %constant.124.clone.1..sunk, s32[]{:T(128)} %get-tuple-element.251, s32[]{:T(128)} %constant.124.clone.1..sunk) | dynamic-update-slice | bytes 1048580 | tf_op jit(solution)/shard_map/while/body/eval_jaxpr/jit(dynamic_update_index_in_dim)/dynamic_update_slice | solution.py:100
  774.9 14.6 %dynamic_update_slice.9 = bf16[2,512,24,128]{3,2,1,0:T(8,128)(2,1)} dynamic-update-slice(bf16[2,512,24,128]{3,2,1,0:T(8,128)(2,1)} %get-tuple-element.252, f32[2,512,1,128]{3,2,1,0:T(1,128)S(1)} %bitcast.109, s32[]{:T(128)} %constant.124.clone.1..sunk, s32[]{:T(128)} %constant.124.clone.1..sunk, s32[]{:T(128)} %get-tuple-element.251, s32[]{:T(128)} %constant.124.clone.1..sunk) | dynamic-update-slice | bytes 1048580 | tf_op jit(solution)/shard_map/while/body/eval_jaxpr/jit(dynamic_update_index_in_dim)/dynamic_update_slice | solution.py:100
  795.6 14.6 %dynamic_update_slice.9 = bf16[2,512,24,128]{3,2,1,0:T(8,128)(2,1)} dynamic-update-slice(bf16[2,512,24,128]{3,2,1,0:T(8,128)(2,1)} %get-tuple-element.252, f32[2,512,1,128]{3,2,1,0:T(1,128)S(1)} %bitcast.109, s32[]{:T(128)} %constant.124.clone.1..sunk, s32[]{:T(128)} %constant.124.clone.1..sunk, s32[]{:T(128)} %get-tuple-element.251, s32[]{:T(128)} %constant.124.clone.1..sunk) | dynamic-update-slice | bytes 1048580 | tf_op jit(solution)/shard_map/while/body/eval_jaxpr/jit(dynamic_update_index_in_dim)/dynamic_update_slice | solution.py:100
  816.3 14.6 %dynamic_update_slice.9 = bf16[2,512,24,128]{3,2,1,0:T(8,128)(2,1)} dynamic-update-slice(bf16[2,512,24,128]{3,2,1,0:T(8,128)(2,1)} %get-tuple-element.252, f32[2,512,1,128]{3,2,1,0:T(1,128)S(1)} %bitcast.109, s32[]{:T(128)} %constant.124.clone.1..sunk, s32[]{:T(128)} %constant.124.clone.1..sunk, s32[]{:T(128)} %get-tuple-element.251, s32[]{:T(128)} %constant.124.clone.1..sunk) | dynamic-update-slice | bytes 1048580 | tf_op jit(solution)/shard_map/while/body/eval_jaxpr/jit(dynamic_update_index_in_dim)/dynamic_update_slice | solution.py:100
  837.0 14.6 %dynamic_update_slice.9 = bf16[2,512,24,128]{3,2,1,0:T(8,128)(2,1)} dynamic-update-slice(bf16[2,512,24,128]{3,2,1,0:T(8,128)(2,1)} %get-tuple-element.252, f32[2,512,1,128]{3,2,1,0:T(1,128)S(1)} %bitcast.109, s32[]{:T(128)} %constant.124.clone.1..sunk, s32[]{:T(128)} %constant.124.clone.1..sunk, s32[]{:T(128)} %get-tuple-element.251, s32[]{:T(128)} %constant.124.clone.1..sunk) | dynamic-update-slice | bytes 1048580 | tf_op jit(solution)/shard_map/while/body/eval_jaxpr/jit(dynamic_update_index_in_dim)/dynamic_update_slice | solution.py:100
  851.6 7.4 copy.63
  859.5 12.1 %all-to-all-start.1 = ((bf16[2,32,16,1,24,128]{5,4,2,0,3,1:T(8,128)(2,1)}), bf16[2,32,16,1,24,128]{5,4,2,0,3,1:T(8,128)(2,1)}, u32[]{:S(2)}, u32[]{:S(2)}) async-start(bf16[2,32,16,1,24,128]{5,4,2,0,3,1:T(8,128)(2,1)} %copy.63), calls=%async_computation.1 | async-start | bytes 12582912 | tf_op jit(solution)/shard_map/all_to_all | solution.py:106
  874.8 40.9 %compare_and_fusion.1 = (pred[544]{0:T(1024)(128)(4,1)S(1)}, s32[544]{0:T(1024)S(1)}) fusion(s32[544]{0:T(1024)S(1)} %copy-done.6, pred[544]{0:T(1024)(128)(4,1)S(1)} %copy-done.7, pred[544]{0:T(1024)(128)(4,1)S(1)} %copy-done.8, pred[544]{0:T(1024)(128)(4,1)S(1)} %copy-done.9, pred[544]{0:T(1024)(128)(4,1)S(1)} %copy-done.10, ...), kind=kLoop, calls=%fused_computation.33 | loop fusion | flops 38080 | bytes 39424 | tf_op jit(solution)/shard_map/jit(_take)/and | solution.py:108
  915.7 91.7 %all-to-all-done.1 = bf16[2,32,16,1,24,128]{5,4,2,0,3,1:T(8,128)(2,1)} async-done(((bf16[2,32,16,1,24,128]{5,4,2,0,3,1:T(8,128)(2,1)}), bf16[2,32,16,1,24,128]{5,4,2,0,3,1:T(8,128)(2,1)}, u32[]{:S(2)}, u32[]{:S(2)}) %all-to-all-start.1) | async-done | bytes 6291488 | tf_op jit(solution)/shard_map/all_to_all | solution.py:106
  1007.3 4.5 copy.64
  1011.9 6.7 copy.65
  1018.6 7.2 gather_fusion.2
  1025.8 3.6 select_bitcast_fusion
  1032.7 5.3 collective-permute-start.3
  1038.0 3.8 copy.70
  1042.7 4.7 multiply_convert_fusion
  1047.4 3.8 copy.71
  (202 shorter events, 111.7 us)
Async XLA Ops:
  0.6 14.6 %copy-start.5 = (f32[544]{0:T(1024)S(1)}, f32[544]{0:T(1024)}, u32[]{:S(2)}) copy-start(f32[544]{0:T(1024)} %constant.145.clone) | copy-start | bytes 6532
  1.7 13.7 %collective-permute-start = (bf16[2,1,544,128]{3,2,1,0:T(8,128)(2,1)S(1)}, bf16[2,1,544,128]{3,2,1,0:T(8,128)(2,1)S(1)}, u32[]{:S(2)}, u32[]{:S(2)}) collective-permute-start(bf16[2,1,544,128]{3,2,1,0:T(8,128)(2,1)S(1)} %get-tuple-element.144), channel_id=1, source_target_pairs={{0,1},{1,2},{2,3},{3,4},{4,5},{5,6},{6,7},{7,8},{8,9},{9,10},{10,1... | collective-permute-start | bytes 835592 | tf_op jit(solution)/shard_map/ppermute | solution.py:24
  5.4 10.4 collective-permute-start.1
  60.6 277.2 %all-to-all-start = ((f32[2,1,16,32,24,128]{5,2,0,4,1,3:T(8,128)}), f32[2,1,16,32,24,128]{5,2,0,4,1,3:T(8,128)}, u32[]{:S(2)}, u32[]{:S(2)}) async-start(f32[2,1,16,32,24,128]{5,2,0,4,1,3:T(8,128)} %broadcast_select_fusion), calls=%async_computation | async-start | bytes 25165824 | tf_op jit(solution)/shard_map/all_to_all | solution.py:90
  68.1 286.0 %copy-start.1 = (bf16[2,2,512,512]{3,2,1,0:T(8,128)(2,1)S(1)}, bf16[2,2,512,512]{3,2,1,0:T(8,128)(2,1)}, u32[]{:S(2)}) copy-start(bf16[2,2,512,512]{3,2,1,0:T(8,128)(2,1)} %param.13) | copy-start | bytes 6291460
  859.0 12.6 %copy-start.2 = (s32[64]{0:T(128)S(1)}, s32[64]{0:T(128)}, u32[]{:S(2)}) copy-start(s32[64]{0:T(128)} %param.15) | copy-start | bytes 772
  859.0 15.4 %copy-start.6 = (s32[544]{0:T(1024)S(1)}, s32[544]{0:T(1024)}, u32[]{:S(2)}) copy-start(s32[544]{0:T(1024)} %constant.150.clone) | copy-start | bytes 6532
  859.0 15.4 %copy-start.7 = (pred[544]{0:T(1024)(128)(4,1)S(1)}, pred[544]{0:T(1024)(128)(4,1)}, u32[]{:S(2)}) copy-start(pred[544]{0:T(1024)(128)(4,1)} %constant.226) | copy-start | bytes 1636
  859.0 15.4 %copy-start.8 = (pred[544]{0:T(1024)(128)(4,1)S(1)}, pred[544]{0:T(1024)(128)(4,1)}, u32[]{:S(2)}) copy-start(pred[544]{0:T(1024)(128)(4,1)} %constant.227) | copy-start | bytes 1636
  859.0 15.4 %copy-start.9 = (pred[544]{0:T(1024)(128)(4,1)S(1)}, pred[544]{0:T(1024)(128)(4,1)}, u32[]{:S(2)}) copy-start(pred[544]{0:T(1024)(128)(4,1)} %constant.228) | copy-start | bytes 1636
  859.0 15.4 %copy-start.10 = (pred[544]{0:T(1024)(128)(4,1)S(1)}, pred[544]{0:T(1024)(128)(4,1)}, u32[]{:S(2)}) copy-start(pred[544]{0:T(1024)(128)(4,1)} %constant.229) | copy-start | bytes 1636
  859.0 15.4 %copy-start.11 = (pred[544]{0:T(1024)(128)(4,1)S(1)}, pred[544]{0:T(1024)(128)(4,1)}, u32[]{:S(2)}) copy-start(pred[544]{0:T(1024)(128)(4,1)} %constant.230) | copy-start | bytes 1636
  859.1 15.4 %copy-start.12 = (pred[544]{0:T(1024)(128)(4,1)S(1)}, pred[544]{0:T(1024)(128)(4,1)}, u32[]{:S(2)}) copy-start(pred[544]{0:T(1024)(128)(4,1)} %constant.231) | copy-start | bytes 1636
  859.1 15.4 %copy-start.13 = (pred[544]{0:T(1024)(128)(4,1)S(1)}, pred[544]{0:T(1024)(128)(4,1)}, u32[]{:S(2)}) copy-start(pred[544]{0:T(1024)(128)(4,1)} %constant.232) | copy-start | bytes 1636
  859.1 15.4 %copy-start.14 = (pred[544]{0:T(1024)(128)(4,1)S(1)}, pred[544]{0:T(1024)(128)(4,1)}, u32[]{:S(2)}) copy-start(pred[544]{0:T(1024)(128)(4,1)} %constant.233) | copy-start | bytes 1636
  859.1 15.4 %copy-start.15 = (pred[544]{0:T(1024)(128)(4,1)S(1)}, pred[544]{0:T(1024)(128)(4,1)}, u32[]{:S(2)}) copy-start(pred[544]{0:T(1024)(128)(4,1)} %constant.234) | copy-start | bytes 1636
  859.1 15.4 %copy-start.16 = (pred[544]{0:T(1024)(128)(4,1)S(1)}, pred[544]{0:T(1024)(128)(4,1)}, u32[]{:S(2)}) copy-start(pred[544]{0:T(1024)(128)(4,1)} %constant.235) | copy-start | bytes 1636
  859.1 15.4 %copy-start.17 = (pred[544]{0:T(1024)(128)(4,1)S(1)}, pred[544]{0:T(1024)(128)(4,1)}, u32[]{:S(2)}) copy-start(pred[544]{0:T(1024)(128)(4,1)} %constant.236) | copy-start | bytes 1636
  859.1 15.4 %copy-start.18 = (pred[544]{0:T(1024)(128)(4,1)S(1)}, pred[544]{0:T(1024)(128)(4,1)}, u32[]{:S(2)}) copy-start(pred[544]{0:T(1024)(128)(4,1)} %constant.237) | copy-start | bytes 1636
  859.1 15.4 %copy-start.19 = (pred[544]{0:T(1024)(128)(4,1)S(1)}, pred[544]{0:T(1024)(128)(4,1)}, u32[]{:S(2)}) copy-start(pred[544]{0:T(1024)(128)(4,1)} %constant.238) | copy-start | bytes 1636
  859.2 15.4 %copy-start.20 = (pred[544]{0:T(1024)(128)(4,1)S(1)}, pred[544]{0:T(1024)(128)(4,1)}, u32[]{:S(2)}) copy-start(pred[544]{0:T(1024)(128)(4,1)} %constant.239) | copy-start | bytes 1636
  859.2 15.4 %copy-start.21 = (pred[544]{0:T(1024)(128)(4,1)S(1)}, pred[544]{0:T(1024)(128)(4,1)}, u32[]{:S(2)}) copy-start(pred[544]{0:T(1024)(128)(4,1)} %constant.240) | copy-start | bytes 1636
  859.2 15.4 %copy-start.22 = (pred[544]{0:T(1024)(128)(4,1)S(1)}, pred[544]{0:T(1024)(128)(4,1)}, u32[]{:S(2)}) copy-start(pred[544]{0:T(1024)(128)(4,1)} %constant.241) | copy-start | bytes 1636
  859.2 15.4 %copy-start.23 = (pred[544]{0:T(1024)(128)(4,1)S(1)}, pred[544]{0:T(1024)(128)(4,1)}, u32[]{:S(2)}) copy-start(pred[544]{0:T(1024)(128)(4,1)} %constant.242) | copy-start | bytes 1636
  859.2 15.4 %copy-start.24 = (pred[544]{0:T(1024)(128)(4,1)S(1)}, pred[544]{0:T(1024)(128)(4,1)}, u32[]{:S(2)}) copy-start(pred[544]{0:T(1024)(128)(4,1)} %constant.243) | copy-start | bytes 1636
  859.2 15.4 %copy-start.25 = (pred[544]{0:T(1024)(128)(4,1)S(1)}, pred[544]{0:T(1024)(128)(4,1)}, u32[]{:S(2)}) copy-start(pred[544]{0:T(1024)(128)(4,1)} %constant.244) | copy-start | bytes 1636
  859.2 15.3 %copy-start.26 = (pred[544]{0:T(1024)(128)(4,1)S(1)}, pred[544]{0:T(1024)(128)(4,1)}, u32[]{:S(2)}) copy-start(pred[544]{0:T(1024)(128)(4,1)} %constant.245) | copy-start | bytes 1636
  859.2 15.3 %copy-start.27 = (pred[544]{0:T(1024)(128)(4,1)S(1)}, pred[544]{0:T(1024)(128)(4,1)}, u32[]{:S(2)}) copy-start(pred[544]{0:T(1024)(128)(4,1)} %constant.246) | copy-start | bytes 1636
  859.3 15.3 %copy-start.28 = (pred[544]{0:T(1024)(128)(4,1)S(1)}, pred[544]{0:T(1024)(128)(4,1)}, u32[]{:S(2)}) copy-start(pred[544]{0:T(1024)(128)(4,1)} %constant.247) | copy-start | bytes 1636
  859.3 15.3 %copy-start.29 = (pred[544]{0:T(1024)(128)(4,1)S(1)}, pred[544]{0:T(1024)(128)(4,1)}, u32[]{:S(2)}) copy-start(pred[544]{0:T(1024)(128)(4,1)} %constant.248) | copy-start | bytes 1636
  859.3 15.3 %copy-start.30 = (pred[544]{0:T(1024)(128)(4,1)S(1)}, pred[544]{0:T(1024)(128)(4,1)}, u32[]{:S(2)}) copy-start(pred[544]{0:T(1024)(128)(4,1)} %constant.249) | copy-start | bytes 1636
  859.3 15.3 %copy-start.31 = (pred[544]{0:T(1024)(128)(4,1)S(1)}, pred[544]{0:T(1024)(128)(4,1)}, u32[]{:S(2)}) copy-start(pred[544]{0:T(1024)(128)(4,1)} %constant.250) | copy-start | bytes 1636
  859.3 15.3 %copy-start.32 = (pred[544]{0:T(1024)(128)(4,1)S(1)}, pred[544]{0:T(1024)(128)(4,1)}, u32[]{:S(2)}) copy-start(pred[544]{0:T(1024)(128)(4,1)} %constant.251) | copy-start | bytes 1636
  859.3 15.3 %copy-start.33 = (pred[544]{0:T(1024)(128)(4,1)S(1)}, pred[544]{0:T(1024)(128)(4,1)}, u32[]{:S(2)}) copy-start(pred[544]{0:T(1024)(128)(4,1)} %constant.252) | copy-start | bytes 1636
  859.3 15.3 %copy-start.34 = (pred[544]{0:T(1024)(128)(4,1)S(1)}, pred[544]{0:T(1024)(128)(4,1)}, u32[]{:S(2)}) copy-start(pred[544]{0:T(1024)(128)(4,1)} %constant.253) | copy-start | bytes 1636
  859.3 15.3 %copy-start.35 = (pred[544]{0:T(1024)(128)(4,1)S(1)}, pred[544]{0:T(1024)(128)(4,1)}, u32[]{:S(2)}) copy-start(pred[544]{0:T(1024)(128)(4,1)} %constant.254) | copy-start | bytes 1636
  859.4 15.3 %copy-start.36 = (pred[544]{0:T(1024)(128)(4,1)S(1)}, pred[544]{0:T(1024)(128)(4,1)}, u32[]{:S(2)}) copy-start(pred[544]{0:T(1024)(128)(4,1)} %constant.255) | copy-start | bytes 1636
  859.4 15.3 %copy-start.37 = (pred[544]{0:T(1024)(128)(4,1)S(1)}, pred[544]{0:T(1024)(128)(4,1)}, u32[]{:S(2)}) copy-start(pred[544]{0:T(1024)(128)(4,1)} %constant.256) | copy-start | bytes 1636
  859.4 15.3 %copy-start.38 = (pred[544]{0:T(1024)(128)(4,1)S(1)}, pred[544]{0:T(1024)(128)(4,1)}, u32[]{:S(2)}) copy-start(pred[544]{0:T(1024)(128)(4,1)} %constant.257) | copy-start | bytes 1636
  859.4 15.3 %copy-start.39 = (pred[544]{0:T(1024)(128)(4,1)S(1)}, pred[544]{0:T(1024)(128)(4,1)}, u32[]{:S(2)}) copy-start(pred[544]{0:T(1024)(128)(4,1)} %constant.258) | copy-start | bytes 1636
  859.4 15.3 %copy-start.40 = (pred[544]{0:T(1024)(128)(4,1)S(1)}, pred[544]{0:T(1024)(128)(4,1)}, u32[]{:S(2)}) copy-start(pred[544]{0:T(1024)(128)(4,1)} %constant.259) | copy-start | bytes 1636
  859.4 15.3 %copy-start.41 = (pred[544]{0:T(1024)(128)(4,1)S(1)}, pred[544]{0:T(1024)(128)(4,1)}, u32[]{:S(2)}) copy-start(pred[544]{0:T(1024)(128)(4,1)} %constant.260) | copy-start | bytes 1636
  859.4 15.3 %copy-start.42 = (pred[544]{0:T(1024)(128)(4,1)S(1)}, pred[544]{0:T(1024)(128)(4,1)}, u32[]{:S(2)}) copy-start(pred[544]{0:T(1024)(128)(4,1)} %constant.261) | copy-start | bytes 1636
  859.4 15.3 %copy-start.43 = (pred[544]{0:T(1024)(128)(4,1)S(1)}, pred[544]{0:T(1024)(128)(4,1)}, u32[]{:S(2)}) copy-start(pred[544]{0:T(1024)(128)(4,1)} %constant.262) | copy-start | bytes 1636
  859.5 15.3 %copy-start.44 = (pred[544]{0:T(1024)(128)(4,1)S(1)}, pred[544]{0:T(1024)(128)(4,1)}, u32[]{:S(2)}) copy-start(pred[544]{0:T(1024)(128)(4,1)} %constant.263) | copy-start | bytes 1636
  859.5 147.9 %all-to-all-start.1 = ((bf16[2,32,16,1,24,128]{5,4,2,0,3,1:T(8,128)(2,1)}), bf16[2,32,16,1,24,128]{5,4,2,0,3,1:T(8,128)(2,1)}, u32[]{:S(2)}, u32[]{:S(2)}) async-start(bf16[2,32,16,1,24,128]{5,4,2,0,3,1:T(8,128)(2,1)} %copy.63), calls=%async_computation.1 | async-start | bytes 12582912 | tf_op jit(solution)/shard_map/all_to_all | solution.py:106
  1030.3 11.5 %collective-permute-start.2 = (bf16[2,1,544,128]{3,2,1,0:T(8,128)(2,1)S(1)}, bf16[2,1,544,128]{3,2,1,0:T(8,128)(2,1)S(1)}, u32[]{:S(2)}, u32[]{:S(2)}) collective-permute-start(bf16[2,1,544,128]{3,2,1,0:T(8,128)(2,1)S(1)} %copy.66), channel_id=1, source_target_pairs={{1,0},{2,1},{3,2},{4,3},{5,4},{6,5},{7,6},{8,7},{9,8},{10,9},{11,1... | collective-permute-start | bytes 835592 | tf_op jit(solution)/shard_map/ppermute | solution.py:25
  1032.7 9.5 collective-permute-start.3
  (6 other events, 39.6 us)
where the time goes:
time: 1070 us; the launch traced here: 1050 us
  local copies, waits for them, and re-layouts  502 us (47%)
  waiting for transfers between devices  361 us (34%)
  other arithmetic  83.6 us (8%)
  loops' own time  46.9 us (4%)
  starting transfers between devices  31.9 us (3%)
  matrix products  24.1 us (2%)
    dynamic_update_slice x24, local copies, waits for them, and re-layouts, solve_slot(): return lax.dynamic_update_index_in_dim(solved, product, slot_index, 2)  350 us
    all_to_all x1, waiting for transfers between devices, body(): lax.all_to_all(outgoing, ('rad', 'lm'), split_axis=3, concat_axis=1, tile...  270 us
    all_to_all x1, waiting for transfers between devices, body(): lax.all_to_all(outgoing_back, ('rad', 'lm'), split_axis=1, concat_axis=3,...  91.7 us
    dynamic_slice x24, local copies, waits for them, and re-layouts, solve_slot(): block_rhs = lax.dynamic_index_in_dim(columns, slot_index, 2, keepdims=False)  62.3 us
    another operation x1, loops' own time, body(): solved = lax.fori_loop(0, capacity, solve_slot, jnp.zeros_like(columns))  46.9 us
    and x1, other arithmetic, body(): new_grid = jnp.take(flat_slots, slot_place, axis=2)  40.9 us
    dot_general x24, matrix products, solve_slot(): jnp.einsum('fij,fjc->fic', matrix, block_rhs, precision=lax.Precision.HIG...  24.1 us
  transfers between devices with their start and end apart: 6, of which 2 were waited for; matrix products, arithmetic and copies ran while one was open for 5% of the time, Pallas kernels for 0%

commit v1 on v0

v1 whole, which is shorter than its diff:
```python
import functools

import jax
import jax.numpy as jnp
import numpy as np
from jax import lax
from jax.experimental import pallas as pl
from jax.experimental.pallas import tpu as pltpu
from jax.sharding import PartitionSpec as P

LMAX1 = 1024
OB = 64
AXES = ("rad", "lm")

inner_radius = 0.35
shell_depth = 0.65
diffusion_numbers = (0.9, 0.4)


class Sizes:
    def __init__(self, devices, grid_field, inverses, slot_blocks):
        self.devices = devices
        self.fields, self.local, self.blocks, self.width = grid_field.shape
        self.levels = inverses.shape[-1]
        self.capacity = slot_blocks.shape[1]
        self.degrees = 2 * devices
        self.spacing = LMAX1 // self.degrees
        self.group_size = OB * self.degrees // LMAX1
        index = np.arange(self.degrees)
        self.counts = [int(c) for c in index // self.group_size + 1]
        self.starts = [int(s) for s in np.cumsum(self.counts) - self.counts]


def transposer(outer, inner):
    size = outer * inner
    row = lax.broadcasted_iota(jnp.int32, (size, size), 0)
    column = lax.broadcasted_iota(jnp.int32, (size, size), 1)
    source = lax.rem(row, inner) * outer + lax.div(row, inner)
    return jnp.where(source == column, 1.0, 0.0).astype(jnp.bfloat16)


def pack_kernel(z, start_ref, field_ref, out_ref, turned_ref):
    rows = 16
    turn = transposer(rows, z.local)

    def group(g, carry):
        at = pl.multiple_of(g * rows, rows)
        part = field_ref[0, :, pl.ds(at, rows), :].reshape(z.local * rows, z.width)
        turned = jnp.dot(turn, part, preferred_element_type=jnp.float32)
        turned_ref[pl.ds(at, rows)] = turned.astype(jnp.bfloat16).reshape(rows, z.local, z.width)
        return carry

    lax.fori_loop(0, z.blocks // rows, group, 0, unroll=2)
    for q in range(z.degrees):
        out_ref[pl.ds(start_ref[q], z.counts[q])] = turned_ref[pl.ds(z.starts[q], z.counts[q])]


def pack(z, start, grid_field, f, slots):
    total = z.devices * slots
    return pl.pallas_call(
        functools.partial(pack_kernel, z),
        grid_spec=pltpu.PrefetchScalarGridSpec(
            num_scalar_prefetch=1,
            grid=(1,),
            in_specs=[
                pl.BlockSpec((1, z.local, z.blocks, z.width), lambda i, start: (f, 0, 0, 0))
            ],
            out_specs=pl.BlockSpec((total, z.local, z.width), lambda i, start: (0, 0, 0)),
            scratch_shapes=[pltpu.VMEM((z.blocks, z.local, z.width), jnp.bfloat16)],
        ),
        out_shape=jax.ShapeDtypeStruct((total, z.local, z.width), jnp.bfloat16),
        compiler_params=pltpu.CompilerParams(vmem_limit_bytes=48 << 20),
        cost_estimate=pl.CostEstimate(flops=10**9, bytes_accessed=10**7, transcendentals=0),
        name=f"pack_{f}",
    )(start, grid_field)


def solve_kernel(z, strength, slots, per_step, start_ref, place_ref, columns_ref, inverse_ref,
                 out_ref, square_ref, above_ref, below_ref, degree_ref, position_ref):
    step = pl.program_id(0)
    shape = (z.levels, z.width)

    @pl.when(step == 0)
    def _():
        level = lax.broadcasted_iota(jnp.int32, shape, 0)

        def radius(positions):
            return inner_radius + shell_depth * (positions + 1).astype(jnp.float32) / (z.levels + 1)

        here = radius(level)
        scaled = (shell_depth / (z.levels + 1)) / here
        square_ref[...] = strength * (scaled * scaled)
        above_ref[...] = jnp.where(level == z.levels - 1, 0.0, strength * radius(level + 1) / here)
        below_ref[...] = jnp.where(level == 0, 0.0, strength * radius(level - 1) / here)
        base = place_ref[0] * slots

        def clear(k, carry):
            degree_ref[k] = 0
            position_ref[k] = 0
            return carry

        lax.fori_loop(0, slots, clear, 0)

        def degree(q, carry):
            first = start_ref[q] - base
            count = lax.div(q, z.group_size) + 1

            def mark(k, inner):
                degree_ref[k] = q
                position_ref[k] = k - first
                return inner

            lax.fori_loop(
                jnp.maximum(first, 0), jnp.minimum(first + count, slots), mark, 0
            )
            return carry

        lax.fori_loop(0, z.degrees, degree, 0)

    column = lax.broadcasted_iota(jnp.int32, shape, 1)
    for k in range(per_step):
        slot = step * per_step + k
        q = degree_ref[slot]
        value = z.spacing * (q + 1) - 1
        upper = jnp.where(q >= z.degrees // 2, 1, 0)
        factor = (value * (value + 1)).astype(jnp.float32)
        limit = 2 * (value - position_ref[slot] * (z.width // 2)) + 1
        u = columns_ref[:, k].reshape(shape).astype(jnp.float32)
        u = jnp.where(column <= limit, u, 0.0)
        weight = (1.0 - 2.0 * strength) - factor * square_ref[...]
        rhs = weight * u
        rhs += above_ref[...] * pltpu.roll(u, z.levels - 1, 0)
        rhs += below_ref[...] * pltpu.roll(u, 1, 0)
        high = rhs.astype(jnp.bfloat16)
        low = (rhs - high.astype(jnp.float32)).astype(jnp.bfloat16)
        both = jnp.concatenate([high, low], axis=1)
        product = jnp.dot(inverse_ref[0, upper], both, preferred_element_type=jnp.float32)
        solved = product[:, : z.width] + product[:, z.width :]
        out_ref[:, k] = solved.astype(jnp.bfloat16).reshape(z.devices, z.local, z.width)


def solve(z, start, place, columns, inverses, f, slots):
    per_step = max(n for n in (1, 2, 3, 4) if slots % n == 0)
    block = (z.devices, per_step, z.local, z.width)
    spec = pl.BlockSpec(block, lambda i, *s: (0, i, 0, 0))
    return pl.pallas_call(
        functools.partial(solve_kernel, z, diffusion_numbers[f], slots, per_step),
        grid_spec=pltpu.PrefetchScalarGridSpec(
            num_scalar_prefetch=2,
            grid=(slots // per_step,),
            in_specs=[
                spec,
                pl.BlockSpec(
                    (1,) + inverses.shape[1:], lambda i, *s: (f, 0, 0, 0)
                ),
            ],
            out_specs=spec,
            scratch_shapes=[pltpu.VMEM((z.levels, z.width), jnp.float32)] * 3
            + [pltpu.SMEM((slots,), jnp.int32)] * 2,
        ),
        out_shape=jax.ShapeDtypeStruct(columns.shape, jnp.bfloat16),
        compiler_params=pltpu.CompilerParams(vmem_limit_bytes=48 << 20),
        cost_estimate=pl.CostEstimate(flops=10**10, bytes_accessed=10**7, transcendentals=0),
        name=f"solve_{f}",
    )(start, place, columns, inverses)


def unpack_kernel(z, start_ref, returned_ref, *rest):
    grid_ref, slope_ref, sorted_ref = rest[-3:]
    rows = 16
    turn = transposer(z.local, rows)
    for q in range(z.degrees):
        sorted_ref[pl.ds(z.starts[q], z.counts[q])] = returned_ref[pl.ds(start_ref[q], z.counts[q])]

    def group(g, carry):
        at = pl.multiple_of(g * rows, rows)
        part = sorted_ref[pl.ds(at, rows)].reshape(rows * z.local, z.width)
        turned = jnp.dot(turn, part, preferred_element_type=jnp.float32)
        turned = turned.reshape(z.local, rows, z.width)
        grid_ref[0, :, pl.ds(at, rows), :] = turned.astype(jnp.bfloat16)
        slope = 0.5 * (turned[2:] - turned[:-2])
        slope_ref[0, pl.ds(1, z.local - 2), pl.ds(at, rows), :] = slope.astype(jnp.bfloat16)
        return carry

    lax.fori_loop(0, z.blocks // rows, group, 0, unroll=2)


def unpack(z, start, returned, f, earlier):
    shape = jax.ShapeDtypeStruct((z.fields, z.local, z.blocks, z.width), jnp.bfloat16)
    spec = pl.BlockSpec((1, z.local, z.blocks, z.width), lambda i, *s: (f, 0, 0, 0))
    return pl.pallas_call(
        functools.partial(unpack_kernel, z),
        grid_spec=pltpu.PrefetchScalarGridSpec(
            num_scalar_prefetch=1,
            grid=(1,),
            in_specs=[pl.BlockSpec(returned.shape, lambda i, *s: (0, 0, 0))]
            + [pl.BlockSpec(memory_space=pl.ANY)] * len(earlier),
            out_specs=[spec, spec],
            scratch_shapes=[pltpu.VMEM((z.blocks, z.local, z.width), jnp.bfloat16)],
        ),
        out_shape=[shape, shape],
        input_output_aliases={2 + i: i for i in range(len(earlier))},
        compiler_params=pltpu.CompilerParams(vmem_limit_bytes=48 << 20),
        cost_estimate=pl.CostEstimate(flops=10**9, bytes_accessed=10**7, transcendentals=0),
        name=f"unpack_{f}",
    )(start, returned, *earlier)


def edge_kernel(slope_in_ref, inside_ref, outside_ref, slope_ref):
    del slope_in_ref
    inside = inside_ref[...].astype(jnp.float32)
    outside = outside_ref[...].astype(jnp.float32).reshape(inside.shape)
    first = pl.program_id(0) == 0
    slope_ref[...] = jnp.where(first, 0.5 * (inside - outside), 0.5 * (outside - inside)).astype(
        jnp.bfloat16
    )


def edges(z, slope, grid, outside, f):
    last = z.local - 1
    block = (1, 1, z.blocks, z.width)
    return pl.pallas_call(
        edge_kernel,
        grid=(2,),
        in_specs=[
            pl.BlockSpec(memory_space=pl.ANY),
            pl.BlockSpec(block, lambda i: (f, 1 + i * (last - 2), 0, 0)),
            pl.BlockSpec((1, z.blocks, z.width), lambda i: (i, 0, 0)),
        ],
        out_specs=pl.BlockSpec(block, lambda i: (f, i * last, 0, 0)),
        out_shape=jax.ShapeDtypeStruct(slope.shape, slope.dtype),
        input_output_aliases={0: 0},
        name=f"edges_{f}",
    )(slope, grid, outside)


def beside(z, first, last):
    up = [(i, i + 1) for i in range(z.devices - 1)]
    down = [(j, i) for i, j in up]
    return lax.ppermute(last, AXES, up), lax.ppermute(first, AXES, down)


def exchange(z, value, slots):
    shaped = value.reshape(z.devices, slots, z.local, z.width)
    return lax.all_to_all(shaped, AXES, split_axis=0, concat_axis=0, tiled=True)


def body(grid_field, inverses, slot_blocks, degree_start):
    devices = lax.axis_size("rad") * lax.axis_size("lm")
    z = Sizes(devices, grid_field, inverses, slot_blocks)
    if z.local % 16:
        return plain_body(z, grid_field, inverses, degree_start)
    slots = z.capacity
    start = degree_start
    place = lax.axis_index(AXES).reshape(1).astype(jnp.int32)
    sent = [pack(z, start, grid_field, f, slots) for f in range(z.fields)]
    columns = [exchange(z, sent[f], slots) for f in range(z.fields)]
    solved = [solve(z, start, place, columns[f], inverses, f, slots) for f in range(z.fields)]
    returned = [
        exchange(z, solved[f], slots).reshape(devices * slots, z.local, z.width)
        for f in range(z.fields)
    ]
    outs = ()
    for f in range(z.fields):
        outs = tuple(unpack(z, start, returned[f], f, outs))
        grid, slope = outs
        before, after = beside(z, grid[f, :1], grid[f, -1:])
        outs = (grid, edges(z, slope, grid, jnp.concatenate([before, after]), f))
    return outs


def plain_body(z, grid_field, inverses, degree_start):
    index = np.arange(z.degrees)
    counts = np.asarray(z.counts)
    degree_of = np.repeat(index, counts)
    place_in = np.arange(z.blocks) - np.asarray(z.starts)[degree_of]
    value = z.spacing * (index + 1) - 1
    slot_place = degree_start[degree_of] + jnp.asarray(place_in, jnp.int32)
    total = z.devices * z.capacity
    holder = jnp.full((total,), z.blocks, jnp.int32)
    holder = holder.at[slot_place].set(jnp.arange(z.blocks, dtype=jnp.int32))
    sent = jnp.take(grid_field, holder, axis=2, mode="fill", fill_value=0)
    sent = sent.reshape(z.fields, z.local, z.devices, z.capacity, z.width)
    columns = lax.all_to_all(sent, AXES, split_axis=2, concat_axis=1, tiled=True)
    columns = columns.reshape(z.fields, z.levels, z.capacity, z.width)
    device = lax.axis_index(AXES)
    mine = lax.dynamic_slice_in_dim(holder, device * z.capacity, z.capacity)
    order = jnp.asarray(place_in)[:, None] * OB + np.arange(z.width)[None, :] // 2
    live_table = (order <= jnp.asarray(value[degree_of])[:, None]).astype(jnp.float32)
    live = jnp.take(live_table, mine, axis=0, mode="fill", fill_value=0)
    factor = (value * (value + 1)).astype(np.float32)[degree_of]
    factor = jnp.take(jnp.asarray(factor), mine, mode="fill", fill_value=0)
    upper = jnp.take(jnp.asarray(degree_of >= z.degrees // 2), mine, mode="fill", fill_value=False)
    radius = inner_radius + shell_depth * jnp.arange(z.levels + 2, dtype=jnp.float32) / (z.levels + 1)
    here = radius[1:-1][None, :, None, None]
    padded = jnp.pad(columns.astype(jnp.float32), ((0, 0), (1, 1), (0, 0), (0, 0)))
    weighted = padded * radius[None, :, None, None]
    second = (weighted[:, 2:] - 2.0 * weighted[:, 1:-1] + weighted[:, :-2]) / here
    scaled = (shell_depth / (z.levels + 1)) / here
    centre = padded[:, 1:-1]
    strength = jnp.asarray(diffusion_numbers, jnp.float32)[:, None, None, None]
    angular = factor[None, None, :, None] * (scaled * scaled) * centre
    rhs = (centre + strength * (second - angular)) * live[None, None]

    def solve_slot(carry, at):
        matrix = lax.dynamic_index_in_dim(
            inverses, upper[at].astype(jnp.int32), 1, keepdims=False
        ).astype(jnp.float32)
        block = lax.dynamic_index_in_dim(rhs, at, 2, keepdims=False)
        product = jnp.einsum("fij,fjc->fic", matrix, block, precision=lax.Precision.HIGHEST)
        return carry, product.astype(jnp.bfloat16)

    solved = lax.scan(solve_slot, 0, jnp.arange(z.capacity))[1]
    solved = jnp.moveaxis(solved, 0, 2)
    solved = solved.reshape(z.fields, z.devices, z.local, z.capacity, z.width)
    returned = lax.all_to_all(solved, AXES, split_axis=1, concat_axis=3, tiled=True)
    returned = returned.reshape(z.fields, z.local, total, z.width)
    grid = jnp.take(returned, slot_place, axis=2)
    before, after = beside(z, grid[:, :1], grid[:, -1:])
    rimmed = jnp.concatenate([before, grid, after], axis=1).astype(jnp.float32)
    return grid, (0.5 * (rimmed[:, 2:] - rimmed[:, :-2])).astype(jnp.bfloat16)


def solution(mesh):
    in_specs = (P(None, AXES), P(None, AXES), P(), P())
    out_specs = (P(None, AXES), P(None, AXES))
    return jax.shard_map(body, mesh=mesh, in_specs=in_specs, out_specs=out_specs, check_vma=False)
```

time: 1070 us -> 341 us (0.32); the launches traced: 1050 us -> 341 us
  local copies, waits for them, and re-layouts: 502 us -> 11.1 us
  waiting for transfers between devices: 361 us -> 238 us
  other arithmetic: 83.6 us -> 1.47 us
  Pallas kernels: 0 us -> 50.3 us
  loops' own time: 46.9 us -> 0 us
  matrix products: 24.1 us -> 0 us
    dynamic_update_slice x24 -> x0, local copies, waits for them, and re-layouts: 350 us -> none  [solve_slot(): return lax.dynamic_update_index_in_dim(solved, product, slot_index, 2)]
    all_to_all x2 -> x4, waiting for transfers between devices: 361 us -> 175 us  [exchange(): return lax.all_to_all(shaped, AXES, split_axis=0, concat_axis=0, tiled=True)]
    dynamic_slice x49 -> x0, local copies, waits for them, and re-layouts: 76.5 us -> none  [the longest x24 62.3 us: solve_slot(): block_rhs = lax.dynamic_index_in_dim(columns, slot_index, 2, keepdims=False)]
    ppermute x4, waiting for transfers between devices: 0.01 us -> 62.9 us  [beside(): return (lax.ppermute(last, AXES, up), lax.ppermute(first, AXES, down))]
    pallas_call x0 -> x8, Pallas kernels: none -> 50.3 us  [the longest x2 17.8 us: solve(): pl.pallas_call(functools.partial(solve_kernel, z, diffusion_numbers[f], s...]
    another operation x1 -> x0, loops' own time: 46.9 us -> none  [body(): solved = lax.fori_loop(0, capacity, solve_slot, jnp.zeros_like(columns))]
    and x2 -> x0, other arithmetic: 41.6 us -> none  [the longest x1 40.9 us: body(): new_grid = jnp.take(flat_slots, slot_place, axis=2)]
    dot_general x24 -> x0, matrix products: 24.1 us -> none  [solve_slot(): jnp.einsum('fij,fjc->fic', matrix, block_rhs, precision=lax.Precision.HIG...]
  transfers between devices with their start and end apart: 6 -> 8, of which waited for: 2 -> 7; matrix products, arithmetic and copies ran while one was open for 5% -> 1% of each run, Pallas kernels for 0% -> 10%
where the time goes in v1:
time: 341 us
  waiting for transfers between devices  238 us (70%)
  Pallas kernels  50.3 us (15%)
  starting transfers between devices  38.8 us (11%)
  local copies, waits for them, and re-layouts  11.1 us (3%)
    all_to_all x4, waiting for transfers between devices, exchange(): return lax.all_to_all(shaped, AXES, split_axis=0, concat_axis=0, tiled=True)  175 us
    ppermute x4, waiting for transfers between devices, beside(): return (lax.ppermute(last, AXES, up), lax.ppermute(first, AXES, down))  62.9 us
    all_to_all x4, starting transfers between devices, exchange(): return lax.all_to_all(shaped, AXES, split_axis=0, concat_axis=0, tiled=True)  26.8 us
    pallas_call x2, Pallas kernels, solve(): pl.pallas_call(functools.partial(solve_kernel, z, diffusion_numbers[f], s...  17.8 us
    pallas_call x2, Pallas kernels, pack(): pl.pallas_call(functools.partial(pack_kernel, z), grid_spec=pltpu.Prefetc...  15.5 us
    pallas_call x2, Pallas kernels, unpack(): pl.pallas_call(functools.partial(unpack_kernel, z), grid_spec=pltpu.Prefe...  13.3 us
    ppermute x4, starting transfers between devices, beside(): return (lax.ppermute(last, AXES, up), lax.ppermute(first, AXES, down))  12 us
    unnamed x16, local copies, waits for them, and re-layouts  9.08 us
  transfers between devices with their start and end apart: 8, of which 7 were waited for; matrix products, arithmetic and copies ran while one was open for 1% of the time, Pallas kernels for 10%

profile of v1, /device:TPU:15, one launch (start us, length us, event | category | flops | bytes accessed | tf_op | source)
XLA Modules:
  0.0 340.7 jit_solution(17740873024002540255)
XLA Ops:
  0.6 0.0 copy-start.4
  0.6 0.6 copy-done.4
  1.3 7.7 %pack_0.1 = bf16[768,16,128]{2,1,0:T(8,128)(2,1)} custom-call(s32[64]{0:T(128)S(1)} %copy-done.4, bf16[2,16,544,128]{3,2,1,0:T(8,128)(2,1)} %field_ref.3), custom_call_target="tpu_custom_call" | custom-call | flops 1000000000 | bytes 10000000 | tf_op jit(solution)/shard_map/pack_0/pallas_call | solution.py:60
  9.0 0.0 copy-start.5
  9.0 6.3 %all-to-all-start.2 = ((bf16[32,24,16,128]{3,2,1,0:T(8,128)(2,1)}), bf16[32,24,16,128]{3,2,1,0:T(8,128)(2,1)}, u32[]{:S(2)}, u32[]{:S(2)}) async-start(bf16[32,24,16,128]{3,2,1,0:T(8,128)(2,1)} %bitcast.3), calls=%async_computation.2 | async-start | bytes 6291456 | tf_op jit(solution)/shard_map/all_to_all | solution.py:245
  15.4 0.0 copy-done.5
  15.4 7.8 %pack_1.1 = bf16[768,16,128]{2,1,0:T(8,128)(2,1)} custom-call(s32[64]{0:T(128)S(1)} %copy-done.5, bf16[2,16,544,128]{3,2,1,0:T(8,128)(2,1)} %field_ref.3), custom_call_target="tpu_custom_call" | custom-call | flops 1000000000 | bytes 10000000 | tf_op jit(solution)/shard_map/pack_1/pallas_call | solution.py:60
  23.1 0.0 copy-start.6
  23.1 60.9 %all-to-all-done.2.columns_ref = bf16[32,24,16,128]{3,2,1,0:T(8,128)(2,1)} async-done(((bf16[32,24,16,128]{3,2,1,0:T(8,128)(2,1)}), bf16[32,24,16,128]{3,2,1,0:T(8,128)(2,1)}, u32[]{:S(2)}, u32[]{:S(2)}) %all-to-all-start.2) | async-done | bytes 3145760 | tf_op jit(solution)/shard_map/all_to_all | solution.py:245
  84.0 6.9 %all-to-all-start = ((bf16[32,24,16,128]{3,2,1,0:T(8,128)(2,1)}), bf16[32,24,16,128]{3,2,1,0:T(8,128)(2,1)}, u32[]{:S(2)}, u32[]{:S(2)}) async-start(bf16[32,24,16,128]{3,2,1,0:T(8,128)(2,1)} %bitcast.1), calls=%async_computation | async-start | bytes 6291456 | tf_op jit(solution)/shard_map/all_to_all | solution.py:245
  90.9 0.0 copy-done.6
  90.9 8.9 %solve_0.1 = bf16[32,24,16,128]{3,2,1,0:T(8,128)(2,1)S(1)} custom-call(s32[64]{0:T(128)S(1)} %copy-done.5, s32[1]{0:T(128)} %bitcast.place_ref, bf16[32,24,16,128]{3,2,1,0:T(8,128)(2,1)} %all-to-all-done.2.columns_ref, bf16[2,2,512,512]{3,2,1,0:T(8,128)(2,1)S(1)} %copy-done.6), custom_call_target="tpu_custom_call" | custom-call | flops 10000000000 | bytes 10000000 | tf_op jit(solution)/shard_map/solve_0/pallas_call | solution.py:146
  99.8 0.0 copy-start.3
  99.8 1.7 copy-done.3
  101.5 58.0 %all-to-all-done.columns_ref = bf16[32,24,16,128]{3,2,1,0:T(8,128)(2,1)} async-done(((bf16[32,24,16,128]{3,2,1,0:T(8,128)(2,1)}), bf16[32,24,16,128]{3,2,1,0:T(8,128)(2,1)}, u32[]{:S(2)}, u32[]{:S(2)}) %all-to-all-start) | async-done | bytes 3145760 | tf_op jit(solution)/shard_map/all_to_all | solution.py:245
  159.5 6.8 %all-to-all-start.3 = ((bf16[32,24,16,128]{3,2,1,0:T(8,128)(2,1)}), bf16[32,24,16,128]{3,2,1,0:T(8,128)(2,1)S(1)}, u32[]{:S(2)}, u32[]{:S(2)}) async-start(bf16[32,24,16,128]{3,2,1,0:T(8,128)(2,1)} %copy-done.3), calls=%async_computation.3 | async-start | bytes 6291456 | tf_op jit(solution)/shard_map/all_to_all | solution.py:245
  166.3 0.0 copy-start.7
  166.3 1.6 copy-done.7
  167.9 8.9 %solve_1.1 = bf16[32,24,16,128]{3,2,1,0:T(8,128)(2,1)S(1)} custom-call(s32[64]{0:T(128)S(1)} %copy-done.5, s32[1]{0:T(128)} %bitcast.place_ref, bf16[32,24,16,128]{3,2,1,0:T(8,128)(2,1)} %all-to-all-done.columns_ref, bf16[2,2,512,512]{3,2,1,0:T(8,128)(2,1)S(1)} %copy-done.7), custom_call_target="tpu_custom_call" | custom-call | flops 10000000000 | bytes 10000000 | tf_op jit(solution)/shard_map/solve_1/pallas_call | solution.py:146
  176.8 0.0 copy-start
  176.8 1.6 copy-done
  178.5 56.5 %all-to-all-done.3 = bf16[32,24,16,128]{3,2,1,0:T(8,128)(2,1)S(1)} async-done(((bf16[32,24,16,128]{3,2,1,0:T(8,128)(2,1)}), bf16[32,24,16,128]{3,2,1,0:T(8,128)(2,1)S(1)}, u32[]{:S(2)}, u32[]{:S(2)}) %all-to-all-start.3) | async-done | bytes 3145760 | tf_op jit(solution)/shard_map/all_to_all | solution.py:245
  235.0 0.0 copy-start.1
  235.0 1.7 copy-done.1
  236.7 6.7 %all-to-all-start.1 = ((bf16[32,24,16,128]{3,2,1,0:T(8,128)(2,1)}), bf16[32,24,16,128]{3,2,1,0:T(8,128)(2,1)S(1)}, u32[]{:S(2)}, u32[]{:S(2)}) async-start(bf16[32,24,16,128]{3,2,1,0:T(8,128)(2,1)} %copy-done), calls=%async_computation.1 | async-start | bytes 6291456 | tf_op jit(solution)/shard_map/all_to_all | solution.py:245
  243.4 0.0 copy-start.2
  243.4 1.9 copy-done.2
  245.3 6.7 %unpack_0.1 = (bf16[2,16,544,128]{3,2,1,0:T(8,128)(2,1)}, bf16[2,16,544,128]{3,2,1,0:T(8,128)(2,1)}) custom-call(s32[64]{0:T(128)S(1)} %copy-done.5, bf16[768,16,128]{2,1,0:T(8,128)(2,1)S(1)} %bitcast.14), custom_call_target="tpu_custom_call" | custom-call | flops 1000000000 | bytes 10000000 | tf_op jit(solution)/shard_map/unpack_0/pallas_call | solution.py:191
  252.0 1.0 slice_bitcast_fusion.3
  253.0 3.3 collective-permute-start
  256.3 1.9 collective-permute-start.1
  258.2 55.3 %collective-permute-done = bf16[1,544,128]{2,1,0:T(8,128)(2,1)S(1)} collective-permute-done((bf16[1,544,128]{2,1,0:T(8,128)(2,1)S(1)}, bf16[1,544,128]{2,1,0:T(8,128)(2,1)S(1)}, u32[]{:S(2)}, u32[]{:S(2)}) %collective-permute-start) | collective-permute-done | bytes 139296 | tf_op jit(solution)/shard_map/ppermute | solution.py:240
  313.5 1.4 collective-permute-done.1
  314.9 0.7 pad_maximum_fusion.outside_ref
  315.6 1.8 edges_0.1.rest_1_
  317.4 0.0 all-to-all-done.1
  317.4 6.7 %unpack_1.1 = (bf16[2,16,544,128]{3,2,1,0:T(8,128)(2,1)}, bf16[2,16,544,128]{3,2,1,0:T(8,128)(2,1)}) custom-call(s32[64]{0:T(128)S(1)} %copy-done.5, bf16[768,16,128]{2,1,0:T(8,128)(2,1)S(1)} %bitcast.13, bf16[2,16,544,128]{3,2,1,0:T(8,128)(2,1)} %get-tuple-element.6.inside_ref.rest_0_, ...), custom_call_target="tpu_custom_call", output_to_operand_aliasing={{0}: (2, {}), {1}: (3, {})} | custom-call | flops 1000000000 | bytes 10000000 | tf_op jit(solution)/shard_map/unpack_1/pallas_call | solution.py:191
  324.1 1.0 slice_bitcast_fusion.1
  325.1 4.8 %collective-permute-start.2 = (bf16[1,544,128]{2,1,0:T(8,128)(2,1)S(1)}, bf16[1,544,128]{2,1,0:T(8,128)(2,1)S(1)}, u32[]{:S(2)}, u32[]{:S(2)}) collective-permute-start(bf16[1,544,128]{2,1,0:T(8,128)(2,1)S(1)} %get-tuple-element.10), channel_id=1, source_target_pairs={{0,1},{1,2},{2,3},{3,4},{4,5},{5,6},{6,7},{7,8},{8,9},{9,10},{10,1... | collective-permute-start | bytes 417800 | tf_op jit(solution)/shard_map/ppermute | solution.py:240
  329.9 1.9 collective-permute-start.3
  331.9 0.1 collective-permute-done.2
  331.9 6.2 %collective-permute-done.3 = bf16[1,544,128]{2,1,0:T(8,128)(2,1)S(1)} collective-permute-done((bf16[1,544,128]{2,1,0:T(8,128)(2,1)S(1)}, bf16[1,544,128]{2,1,0:T(8,128)(2,1)S(1)}, u32[]{:S(2)}, u32[]{:S(2)}) %collective-permute-start.3) | collective-permute-done | bytes 139296 | tf_op jit(solution)/shard_map/ppermute | solution.py:240
  338.1 0.7 pad_maximum_fusion.1.outside_ref
  338.8 1.8 edges_1.1
Async XLA Ops:
  0.6 0.7 copy-start.4
  9.0 6.3 %copy-start.5 = (s32[64]{0:T(128)S(1)}, s32[64]{0:T(128)}, u32[]{:S(2)}) copy-start(s32[64]{0:T(128)} %start_ref.11) | copy-start | bytes 772
  9.0 74.9 %all-to-all-start.2 = ((bf16[32,24,16,128]{3,2,1,0:T(8,128)(2,1)}), bf16[32,24,16,128]{3,2,1,0:T(8,128)(2,1)}, u32[]{:S(2)}, u32[]{:S(2)}) async-start(bf16[32,24,16,128]{3,2,1,0:T(8,128)(2,1)} %bitcast.3), calls=%async_computation.2 | async-start | bytes 6291456 | tf_op jit(solution)/shard_map/all_to_all | solution.py:245
  23.1 67.8 %copy-start.6 = (bf16[2,2,512,512]{3,2,1,0:T(8,128)(2,1)S(1)}, bf16[2,2,512,512]{3,2,1,0:T(8,128)(2,1)}, u32[]{:S(2)}) copy-start(bf16[2,2,512,512]{3,2,1,0:T(8,128)(2,1)} %inverse_ref.3) | copy-start | bytes 6291460
  84.0 75.5 %all-to-all-start = ((bf16[32,24,16,128]{3,2,1,0:T(8,128)(2,1)}), bf16[32,24,16,128]{3,2,1,0:T(8,128)(2,1)}, u32[]{:S(2)}, u32[]{:S(2)}) async-start(bf16[32,24,16,128]{3,2,1,0:T(8,128)(2,1)} %bitcast.1), calls=%async_computation | async-start | bytes 6291456 | tf_op jit(solution)/shard_map/all_to_all | solution.py:245
  99.8 1.7 copy-start.3
  159.5 75.5 %all-to-all-start.3 = ((bf16[32,24,16,128]{3,2,1,0:T(8,128)(2,1)}), bf16[32,24,16,128]{3,2,1,0:T(8,128)(2,1)S(1)}, u32[]{:S(2)}, u32[]{:S(2)}) async-start(bf16[32,24,16,128]{3,2,1,0:T(8,128)(2,1)} %copy-done.3), calls=%async_computation.3 | async-start | bytes 6291456 | tf_op jit(solution)/shard_map/all_to_all | solution.py:245
  166.3 1.6 copy-start.7
  176.8 1.6 copy-start
  235.0 1.7 copy-start.1
  236.7 80.8 %all-to-all-start.1 = ((bf16[32,24,16,128]{3,2,1,0:T(8,128)(2,1)}), bf16[32,24,16,128]{3,2,1,0:T(8,128)(2,1)S(1)}, u32[]{:S(2)}, u32[]{:S(2)}) async-start(bf16[32,24,16,128]{3,2,1,0:T(8,128)(2,1)} %copy-done), calls=%async_computation.1 | async-start | bytes 6291456 | tf_op jit(solution)/shard_map/all_to_all | solution.py:245
  243.4 1.9 copy-start.2
  253.0 60.5 %collective-permute-start = (bf16[1,544,128]{2,1,0:T(8,128)(2,1)S(1)}, bf16[1,544,128]{2,1,0:T(8,128)(2,1)S(1)}, u32[]{:S(2)}, u32[]{:S(2)}) collective-permute-start(bf16[1,544,128]{2,1,0:T(8,128)(2,1)S(1)} %get-tuple-element.12), channel_id=1, source_target_pairs={{0,1},{1,2},{2,3},{3,4},{4,5},{5,6},{6,7},{7,8},{8,9},{9,10},{10,1... | collective-permute-start | bytes 417800 | tf_op jit(solution)/shard_map/ppermute | solution.py:240
  256.3 58.6 %collective-permute-start.1 = (bf16[1,544,128]{2,1,0:T(8,128)(2,1)S(1)}, bf16[1,544,128]{2,1,0:T(8,128)(2,1)S(1)}, u32[]{:S(2)}, u32[]{:S(2)}) collective-permute-start(bf16[1,544,128]{2,1,0:T(8,128)(2,1)S(1)} %get-tuple-element.13), channel_id=1, source_target_pairs={{1,0},{2,1},{3,2},{4,3},{5,4},{6,5},{7,6},{8,7},{9,8},{10,9},{11,1... | collective-permute-start | bytes 417800 | tf_op jit(solution)/shard_map/ppermute | solution.py:240
  325.1 6.8 %collective-permute-start.2 = (bf16[1,544,128]{2,1,0:T(8,128)(2,1)S(1)}, bf16[1,544,128]{2,1,0:T(8,128)(2,1)S(1)}, u32[]{:S(2)}, u32[]{:S(2)}) collective-permute-start(bf16[1,544,128]{2,1,0:T(8,128)(2,1)S(1)} %get-tuple-element.10), channel_id=1, source_target_pairs={{0,1},{1,2},{2,3},{3,4},{4,5},{5,6},{6,7},{7,8},{8,9},{9,10},{10,1... | collective-permute-start | bytes 417800 | tf_op jit(solution)/shard_map/ppermute | solution.py:240
  329.9 8.2 %collective-permute-start.3 = (bf16[1,544,128]{2,1,0:T(8,128)(2,1)S(1)}, bf16[1,544,128]{2,1,0:T(8,128)(2,1)S(1)}, u32[]{:S(2)}, u32[]{:S(2)}) collective-permute-start(bf16[1,544,128]{2,1,0:T(8,128)(2,1)S(1)} %get-tuple-element.11), channel_id=1, source_target_pairs={{1,0},{2,1},{3,2},{4,3},{5,4},{6,5},{7,6},{8,7},{9,8},{10,9},{11,1... | collective-permute-start | bytes 417800 | tf_op jit(solution)/shard_map/ppermute | solution.py:240
